TPU v7x, 128 devices: a whole 4x4x4 slice. The times are simulated.
128 devices in a mesh: seq: 4 (over x_hi, core), fsdp: 32 (over z, x_lo, y).
Axes of the slice: x: 4 (x_hi: 2, x_lo: 2; x = x_hi * 2 + x_lo), y: 4, z: 4, core: 2. Of those that a mesh axis runs over, the one named last changes fastest.
Arguments:
- hidden_states: bfloat16 [32, 2048, 768], P('fsdp', 'seq'), may hold values from -6 to 6
- positions: int32 [32, 2048], P('fsdp', 'seq'), may hold values from 0 to 4095, as said below
- documents: int32 [32, 2048], P('fsdp', 'seq'), may hold values from 0 to 4, as said below
- cotangent: bfloat16 [32, 2048, 768], P('fsdp', 'seq'), may hold values from -6 to 6
- first_gain: bfloat16 [768], P('fsdp'), may hold values from 0.099609375 to 1.8984375
- first_shift: bfloat16 [768], P('fsdp'), may hold values from -1.75 to 1.75
- second_gain: bfloat16 [768], P('fsdp'), may hold values from 0.099609375 to 1.8984375
- second_shift: bfloat16 [768], P('fsdp'), may hold values from -1.75 to 1.75
- joint_weight: bfloat16 [768, 2304], P('fsdp'), may hold values from -0.21875 to 0.21875
- joint_bias: bfloat16 [2304], P('fsdp'), may hold values from -1.75 to 1.75
- output_weight: bfloat16 [768, 768], P('fsdp'), may hold values from -6 to 6
- output_bias: bfloat16 [768], P('fsdp'), may hold values from -1.75 to 1.75
- up_weight: bfloat16 [768, 3072], P('fsdp'), may hold values from -0.21875 to 0.21875
- up_bias: bfloat16 [3072], P('fsdp'), may hold values from -3 to 3
- down_weight: bfloat16 [3072, 768], P('fsdp'), may hold values from -0.109375 to 0.109375
- down_bias: bfloat16 [768], P('fsdp'), may hold values from -1.75 to 1.75
Outputs:
- layer_output: bfloat16 [32, 2048, 768], P('fsdp', 'seq')
- input_grad: bfloat16 [32, 2048, 768], P('fsdp', 'seq')
- first_gain_grad: float32 [768], P('fsdp')
- first_shift_grad: float32 [768], P('fsdp')
- second_gain_grad: float32 [768], P('fsdp')
- second_shift_grad: float32 [768], P('fsdp')
- joint_weight_grad: float32 [768, 2304], P('fsdp')
- joint_bias_grad: float32 [2304], P('fsdp')
- output_weight_grad: float32 [768, 768], P('fsdp')
- output_bias_grad: float32 [768], P('fsdp')
- up_weight_grad: float32 [768, 3072], P('fsdp')
- up_bias_grad: float32 [3072], P('fsdp')
- down_weight_grad: float32 [3072, 768], P('fsdp')
- down_bias_grad: float32 [768], P('fsdp')
Inputs may be any that keep to these rules, and one draw needn't show every extreme that they name: `documents`: within a sequence document numbers never fall; in every sequence one document begins among the tokens of the first device along seq and ends among those of the last. `positions`: A token's position is its place in its document plus an offset for that document; the last token of every sequence holds the largest position.
All inputs are finite; a program needn't handle non-finite values.
Results may differ from a plain program's by a relative error of at most 0.025.
Values may be sent and summed in bfloat16 or wider, within the bound.
A program may use at most 192 MiB of HBM per device.

v0:
```python
import jax
import jax.numpy as jnp
from jax import lax
from jax.sharding import PartitionSpec as P

HEADS = 12
HEAD_DIM = 64
ROT = 16


def norm_parts(states, norm_gain, norm_shift):
    average = jnp.mean(states, axis=-1, keepdims=True)
    centered = states - average
    spread = jnp.mean(centered * centered, axis=-1, keepdims=True)
    return centered * lax.rsqrt(spread + 1e-05) * norm_gain + norm_shift


def scaled_norm(states, norm_gain):
    return norm_parts(states, norm_gain, 0.0)


def gelu_exact(values):
    return jax.nn.gelu(values, approximate=False)


def angles(places):
    freqs = 10000.0 ** (-jnp.arange(0, ROT, 2).astype(jnp.float32) / ROT)
    turned = places.astype(jnp.float32)[:, None] * freqs[None, :]
    return (jnp.cos(turned)[:, None, :], jnp.sin(turned)[:, None, :])


def rotate(values, cosine, sine):
    half_rot = ROT // 2
    first_half = values[..., :half_rot]
    second_half = values[..., half_rot:ROT]
    return jnp.concatenate(
        [
            first_half * cosine - second_half * sine,
            second_half * cosine + first_half * sine,
            values[..., ROT:],
        ],
        axis=-1,
    )


def rotate_back(grads, cosine, sine):
    half_rot = ROT // 2
    first_half = grads[..., :half_rot]
    second_half = grads[..., half_rot:ROT]
    return jnp.concatenate(
        [
            first_half * cosine + second_half * sine,
            second_half * cosine - first_half * sine,
            grads[..., ROT:],
        ],
        axis=-1,
    )


def body(
    hidden_states,
    positions,
    documents,
    cotangent,
    first_gain,
    first_shift,
    second_gain,
    second_shift,
    joint_weight,
    joint_bias,
    output_weight,
    output_bias,
    up_weight,
    up_bias,
    down_weight,
    down_bias,
):
    groups = lax.axis_size("seq")
    model_width = hidden_states.shape[2]
    local_rows = hidden_states.shape[1]
    seq_length = local_rows * groups
    heads_here = HEADS // groups
    group_width = model_width // groups
    block_rows = min(512, seq_length)
    score_scale = HEAD_DIM ** (-0.5)
    gathered = (
        lax.all_gather(first_gain, "fsdp", axis=0, tiled=True),
        lax.all_gather(first_shift, "fsdp", axis=0, tiled=True),
        lax.all_gather(second_gain, "fsdp", axis=0, tiled=True),
        lax.all_gather(second_shift, "fsdp", axis=0, tiled=True),
        lax.all_gather(joint_weight, "fsdp", axis=0, tiled=True),
        lax.all_gather(joint_bias, "fsdp", axis=0, tiled=True),
        lax.all_gather(output_weight, "fsdp", axis=0, tiled=True),
        lax.all_gather(output_bias, "fsdp", axis=0, tiled=True),
        lax.all_gather(up_weight, "fsdp", axis=0, tiled=True),
        lax.all_gather(up_bias, "fsdp", axis=0, tiled=True),
        lax.all_gather(down_weight, "fsdp", axis=0, tiled=True),
        lax.all_gather(down_bias, "fsdp", axis=0, tiled=True),
    )
    (
        gain_one,
        shift_one,
        gain_two,
        shift_two,
        joint_full,
        joint_shift,
        output_full,
        output_shift,
        up_full,
        up_shift,
        down_full,
        down_shift,
    ) = gathered
    states = hidden_states[0].astype(jnp.float32)
    first_in = norm_parts(
        states, gain_one.astype(jnp.float32), shift_one.astype(jnp.float32)
    ).astype(jnp.bfloat16)
    second_in = norm_parts(
        states, gain_two.astype(jnp.float32), shift_two.astype(jnp.float32)
    ).astype(jnp.bfloat16)
    projected = jnp.dot(
        first_in, joint_full, preferred_element_type=jnp.float32
    ) + joint_shift.astype(jnp.float32)
    cosine, sine = angles(positions[0])
    queries = rotate(
        projected[:, :model_width].reshape(local_rows, HEADS, HEAD_DIM), cosine, sine
    ).reshape(local_rows, model_width)
    key_part = rotate(
        projected[:, model_width : 2 * model_width].reshape(local_rows, HEADS, HEAD_DIM),
        cosine,
        sine,
    ).reshape(local_rows, model_width)
    stacked = jnp.stack([queries, key_part, projected[:, 2 * model_width :]]).astype(jnp.bfloat16)
    head_view = lax.all_to_all(stacked, "seq", split_axis=2, concat_axis=1, tiled=True)
    labels = lax.all_gather(documents[0], "seq", axis=0, tiled=True)
    query_heads = head_view[0].reshape(seq_length, heads_here, HEAD_DIM)
    key_heads = head_view[1].reshape(seq_length, heads_here, HEAD_DIM)
    value_heads = head_view[2].reshape(seq_length, heads_here, HEAD_DIM)
    columns = jnp.arange(seq_length, dtype=jnp.int32)

    def masked_scores(offset):
        finish = offset + block_rows
        query_block = query_heads[offset:finish]
        scores = (
            jnp.einsum(
                "qhd,khd->hqk", query_block, key_heads[:finish], preferred_element_type=jnp.float32
            )
            * score_scale
        )
        allowed = (columns[offset:finish, None] >= columns[None, :finish]) & (
            labels[offset:finish, None] == labels[None, :finish]
        )
        return jnp.where(allowed[None], scores, -1e30)

    outputs = []
    log_sums = []
    for offset in range(0, seq_length, block_rows):
        finish = offset + block_rows
        scores = masked_scores(offset)
        row_peak = jnp.max(scores, axis=-1, keepdims=True)
        exponent = jnp.exp(scores - row_peak)
        row_total = jnp.sum(exponent, axis=-1, keepdims=True)
        probs_low = (exponent / row_total).astype(jnp.bfloat16)
        outputs.append(
            jnp.einsum(
                "hqk,khd->qhd", probs_low, value_heads[:finish], preferred_element_type=jnp.float32
            )
        )
        log_sums.append(row_peak + jnp.log(row_total))
    context_heads = (
        jnp.concatenate(outputs, axis=0).reshape(seq_length, group_width).astype(jnp.bfloat16)
    )
    context = lax.all_to_all(context_heads, "seq", split_axis=0, concat_axis=1, tiled=True)
    attn_out = jnp.dot(
        context, output_full, preferred_element_type=jnp.float32
    ) + output_shift.astype(jnp.float32)
    hidden_pre = jnp.dot(second_in, up_full, preferred_element_type=jnp.float32) + up_shift.astype(
        jnp.float32
    )
    activated, gelu_pull = jax.vjp(gelu_exact, hidden_pre)
    act_low = activated.astype(jnp.bfloat16)
    mlp_out = jnp.dot(act_low, down_full, preferred_element_type=jnp.float32) + down_shift.astype(
        jnp.float32
    )
    layer_output = (states + attn_out + mlp_out).astype(jnp.bfloat16)
    backward = (
        lax.all_gather(first_gain, "fsdp", axis=0, tiled=True),
        lax.all_gather(second_gain, "fsdp", axis=0, tiled=True),
        lax.all_gather(joint_weight, "fsdp", axis=0, tiled=True),
        lax.all_gather(output_weight, "fsdp", axis=0, tiled=True),
        lax.all_gather(up_weight, "fsdp", axis=0, tiled=True),
        lax.all_gather(down_weight, "fsdp", axis=0, tiled=True),
    )
    gain_one_back, gain_two_back, joint_back, output_back, up_back, down_back = backward
    tangent = cotangent[0]
    tangent_wide = tangent.astype(jnp.float32)
    bias_sum = jnp.sum(tangent_wide, axis=0)
    down_weight_grad = jnp.einsum("tf,td->fd", act_low, tangent, preferred_element_type=jnp.float32)
    act_grad = jnp.einsum("td,fd->tf", tangent, down_back, preferred_element_type=jnp.float32)
    hidden_grad = gelu_pull(act_grad)[0].astype(jnp.bfloat16)
    up_weight_grad = jnp.einsum(
        "td,tf->df", second_in, hidden_grad, preferred_element_type=jnp.float32
    )
    up_bias_grad = jnp.sum(hidden_grad.astype(jnp.float32), axis=0)
    second_grad = jnp.einsum("tf,df->td", hidden_grad, up_back, preferred_element_type=jnp.float32)
    output_weight_grad = jnp.einsum(
        "td,te->de", context, tangent, preferred_element_type=jnp.float32
    )
    context_grad = jnp.einsum(
        "te,de->td", tangent, output_back, preferred_element_type=jnp.float32
    ).astype(jnp.bfloat16)
    grad_heads = lax.all_to_all(
        context_grad, "seq", split_axis=1, concat_axis=0, tiled=True
    ).reshape(seq_length, heads_here, HEAD_DIM)
    query_grads = []
    key_grad = jnp.zeros((seq_length, heads_here, HEAD_DIM), jnp.float32)
    value_grad = jnp.zeros((seq_length, heads_here, HEAD_DIM), jnp.float32)
    for block_index, offset in enumerate(range(0, seq_length, block_rows)):
        finish = offset + block_rows
        scores = masked_scores(offset)
        probs = jnp.exp(scores - log_sums[block_index])
        probs_low = probs.astype(jnp.bfloat16)
        grad_block = grad_heads[offset:finish]
        value_grad = value_grad.at[:finish].add(
            jnp.einsum("hqk,qhd->khd", probs_low, grad_block, preferred_element_type=jnp.float32)
        )
        prob_grad = jnp.einsum(
            "qhd,khd->hqk", grad_block, value_heads[:finish], preferred_element_type=jnp.float32
        )
        weighted = jnp.sum(probs * prob_grad, axis=-1, keepdims=True)
        score_grad = (probs * (prob_grad - weighted)).astype(jnp.bfloat16)
        query_grads.append(
            jnp.einsum(
                "hqk,khd->qhd", score_grad, key_heads[:finish], preferred_element_type=jnp.float32
            )
            * score_scale
        )
        key_grad = key_grad.at[:finish].add(
            jnp.einsum(
                "hqk,qhd->khd",
                score_grad,
                query_heads[offset:finish],
                preferred_element_type=jnp.float32,
            )
            * score_scale
        )
    head_grads = jnp.stack(
        [
            jnp.concatenate(query_grads, axis=0).reshape(seq_length, group_width),
            key_grad.reshape(seq_length, group_width),
            value_grad.reshape(seq_length, group_width),
        ]
    ).astype(jnp.bfloat16)
    token_grads = lax.all_to_all(head_grads, "seq", split_axis=1, concat_axis=2, tiled=True)
    query_back = rotate_back(
        token_grads[0].astype(jnp.float32).reshape(local_rows, HEADS, HEAD_DIM), cosine, sine
    ).reshape(local_rows, model_width)
    key_back = rotate_back(
        token_grads[1].astype(jnp.float32).reshape(local_rows, HEADS, HEAD_DIM), cosine, sine
    ).reshape(local_rows, model_width)
    joint_grad = jnp.concatenate(
        [query_back, key_back, token_grads[2].astype(jnp.float32)], axis=1
    ).astype(jnp.bfloat16)
    joint_weight_grad = jnp.einsum(
        "td,tc->dc", first_in, joint_grad, preferred_element_type=jnp.float32
    )
    joint_bias_grad = jnp.sum(joint_grad.astype(jnp.float32), axis=0)
    first_grad = jnp.einsum("tc,dc->td", joint_grad, joint_back, preferred_element_type=jnp.float32)
    unused_one, first_pull = jax.vjp(scaled_norm, states, gain_one_back.astype(jnp.float32))
    first_term, gain_one_grad = first_pull(first_grad)
    unused_two, second_pull = jax.vjp(scaled_norm, states, gain_two_back.astype(jnp.float32))
    second_term, gain_two_grad = second_pull(second_grad)
    shift_one_grad = jnp.sum(first_grad, axis=0)
    shift_two_grad = jnp.sum(second_grad, axis=0)
    input_grad = (tangent_wide + first_term + second_term).astype(jnp.bfloat16)
    shares = (
        lax.psum_scatter(
            gain_one_grad.astype(jnp.bfloat16), "fsdp", scatter_dimension=0, tiled=True
        ).astype(jnp.float32),
        lax.psum_scatter(
            shift_one_grad.astype(jnp.bfloat16), "fsdp", scatter_dimension=0, tiled=True
        ).astype(jnp.float32),
        lax.psum_scatter(
            gain_two_grad.astype(jnp.bfloat16), "fsdp", scatter_dimension=0, tiled=True
        ).astype(jnp.float32),
        lax.psum_scatter(
            shift_two_grad.astype(jnp.bfloat16), "fsdp", scatter_dimension=0, tiled=True
        ).astype(jnp.float32),
        lax.psum_scatter(
            joint_weight_grad.astype(jnp.bfloat16), "fsdp", scatter_dimension=0, tiled=True
        ).astype(jnp.float32),
        lax.psum_scatter(
            joint_bias_grad.astype(jnp.bfloat16), "fsdp", scatter_dimension=0, tiled=True
        ).astype(jnp.float32),
        lax.psum_scatter(
            output_weight_grad.astype(jnp.bfloat16), "fsdp", scatter_dimension=0, tiled=True
        ).astype(jnp.float32),
        lax.psum_scatter(
            bias_sum.astype(jnp.bfloat16), "fsdp", scatter_dimension=0, tiled=True
        ).astype(jnp.float32),
        lax.psum_scatter(
            up_weight_grad.astype(jnp.bfloat16), "fsdp", scatter_dimension=0, tiled=True
        ).astype(jnp.float32),
        lax.psum_scatter(
            up_bias_grad.astype(jnp.bfloat16), "fsdp", scatter_dimension=0, tiled=True
        ).astype(jnp.float32),
        lax.psum_scatter(
            down_weight_grad.astype(jnp.bfloat16), "fsdp", scatter_dimension=0, tiled=True
        ).astype(jnp.float32),
        lax.psum_scatter(
            bias_sum.astype(jnp.bfloat16), "fsdp", scatter_dimension=0, tiled=True
        ).astype(jnp.float32),
    )
    summed = (
        lax.psum(shares[0].astype(jnp.bfloat16), "seq").astype(jnp.float32),
        lax.psum(shares[1].astype(jnp.bfloat16), "seq").astype(jnp.float32),
        lax.psum(shares[2].astype(jnp.bfloat16), "seq").astype(jnp.float32),
        lax.psum(shares[3].astype(jnp.bfloat16), "seq").astype(jnp.float32),
        lax.psum(shares[4].astype(jnp.bfloat16), "seq").astype(jnp.float32),
        lax.psum(shares[5].astype(jnp.bfloat16), "seq").astype(jnp.float32),
        lax.psum(shares[6].astype(jnp.bfloat16), "seq").astype(jnp.float32),
        lax.psum(shares[7].astype(jnp.bfloat16), "seq").astype(jnp.float32),
        lax.psum(shares[8].astype(jnp.bfloat16), "seq").astype(jnp.float32),
        lax.psum(shares[9].astype(jnp.bfloat16), "seq").astype(jnp.float32),
        lax.psum(shares[10].astype(jnp.bfloat16), "seq").astype(jnp.float32),
        lax.psum(shares[11].astype(jnp.bfloat16), "seq").astype(jnp.float32),
    )
    return (
        layer_output[None],
        input_grad[None],
        summed[0],
        summed[1],
        summed[2],
        summed[3],
        summed[4],
        summed[5],
        summed[6],
        summed[7],
        summed[8],
        summed[9],
        summed[10],
        summed[11],
    )


def solution(mesh):
    in_specs = (
        P("fsdp", "seq", None),
        P("fsdp", "seq"),
        P("fsdp", "seq"),
        P("fsdp", "seq", None),
        P("fsdp"),
        P("fsdp"),
        P("fsdp"),
        P("fsdp"),
        P("fsdp", None),
        P("fsdp"),
        P("fsdp", None),
        P("fsdp"),
        P("fsdp", None),
        P("fsdp"),
        P("fsdp", None),
        P("fsdp"),
    )
    out_specs = (
        P("fsdp", "seq", None),
        P("fsdp", "seq", None),
        P("fsdp"),
        P("fsdp"),
        P("fsdp"),
        P("fsdp"),
        P("fsdp", None),
        P("fsdp"),
        P("fsdp", None),
        P("fsdp"),
        P("fsdp", None),
        P("fsdp"),
        P("fsdp", None),
        P("fsdp"),
    )
    return jax.shard_map(body, mesh=mesh, in_specs=in_specs, out_specs=out_specs, check_vma=False)
```

profile of v0, /device:TPU:1, one launch (start us, length us, event | category | flops | bytes accessed | tf_op | source)
XLA Modules:
  0.0 1372.3 jit_solution(12503517465756184570)
XLA Ops:
  10.0 8.0 all-gather
  30.0 133.6 %all-reduce.18 = (bf16[768]{0:T(1024)(128)(2,1)}, bf16[768]{0:T(1024)(128)(2,1)}, bf16[3072]{0:T(1024)(128)(2,1)}, bf16[2304]{0:T(1024)(128)(2,1)S(1)}, bf16[768...) all-reduce(bf16[768]{0:T(1024)(128)(2,1)S(1)} %dynamic-update-slice.27, ...), channel_id=1, replica_groups=mesh['seq'=4,'fsdp'=32] {'fsdp'}, use_global_device_ids=true, to_apply=%add.7 | all-reduce | flops 8448 | bytes 33792
  167.4 30.5 %all-to-all-start.2 = ((bf16[512,4,192]{0,2,1:T(8,128)(2,1)}), bf16[512,4,192]{0,2,1:T(8,128)(2,1)}, u32[]{:S(2)}, u32[]{:S(2)}) async-start(bf16[512,4,192]{0,2,1:T(8,128)(2,1)} %bitcast.33), calls=%async_computation.2 | async-start | bytes 1572864 | tf_op jit(solution)/shard_map/all_to_all | solution.py:212
  197.9 106.6 %all-gather.6.cloned.1.call-done = bf16[768,2304]{1,0:T(8,128)(2,1)} async-done(((bf16[24,2304]{1,0:T(8,128)(2,1)}), bf16[768,2304]{1,0:T(8,128)(2,1)}) %all-gather.6.cloned.1.call-update) | async-done | bytes 3538960 | tf_op jit(solution)/shard_map/all_gather | solution.py:91
  304.5 4.2 convolution_add_fusion
  322.1 4.3 copy.92
  326.5 24.6 %all-to-all-start = ((bf16[3,512,768]{1,0,2:T(4,128)(2,1)}), bf16[3,512,768]{1,0,2:T(4,128)(2,1)S(1)}, u32[]{:S(2)}, u32[]{:S(2)}) async-start(bf16[3,512,768]{1,0,2:T(4,128)(2,1)} %copy.92), calls=%async_computation | async-start | bytes 6291456 | tf_op jit(solution)/shard_map/all_to_all | solution.py:134
  359.2 45.8 %all-to-all-done = bf16[3,512,768]{1,0,2:T(4,128)(2,1)S(1)} async-done(((bf16[3,512,768]{1,0,2:T(4,128)(2,1)}), bf16[3,512,768]{1,0,2:T(4,128)(2,1)S(1)}, u32[]{:S(2)}, u32[]{:S(2)}) %all-to-all-start) | async-done | bytes 2359328 | tf_op jit(solution)/shard_map/all_to_all | solution.py:134
  429.5 3.8 multiply_reduce_fusion.2
  439.0 4.7 multiply_reduce_fusion.1
  443.7 2.7 fusion.142
  448.4 5.2 multiply_convert_fusion.4
  453.6 8.2 multiply_convert_fusion.2
  461.9 8.0 multiply_convert_fusion.1
  469.9 3.0 fusion.46
  474.9 5.9 copy.108
  480.8 3.9 fusion.90
  484.7 5.5 fusion.28
  490.1 4.2 multiply_reduce_fusion
  494.4 4.5 multiply_convert_fusion
  498.9 5.0 fusion.49
  503.9 5.9 copy.107
  511.7 3.0 fusion.107
  514.7 3.9 fusion.109
  518.7 4.8 fusion.106
  524.5 5.9 copy.106
  530.4 9.4 pad_maximum_fusion
  539.8 74.8 %all_to_all.62 = bf16[3,2048,192]{2,0,1:T(4,128)(2,1)} all-to-all(bf16[3,2048,192]{2,0,1:T(4,128)(2,1)S(1)} %pad_maximum_fusion), channel_id=1, replica_groups=mesh['seq'=4,'fsdp'=32] {'seq'}, dimensions={1} | all-to-all | bytes 4718592 | tf_op jit(solution)/shard_map/all_to_all | solution.py:254
  614.6 7.5 copy.117
  627.0 4.2 convolution_convert_fusion.2
  631.9 20.0 %multiply_convert_fusion.3 = (bf16[512,3072]{1,0:T(8,128)(2,1)}, f32[512,3072]{1,0:T(8,128)}, f32[512,3072]{1,0:T(8,128)}) fusion(f32[3072]{0:T(1024)S(1)} %convert_element_type.241, bf16[768,3072]{1,0:T(8,128)(2,1)} %all-gather.10.cloned.1.call-done, bf16[1,512,768]{2,1,0:T(8,128)(2,1)} %param.36, f32[768]{0:T(1024)S(1)} %convert_element_type.239, ...), kind=kOutput, calls=%fused_computation.24 | convolution fusion | flops 2522087424 | bytes 21256192 | tf_op jit(solution)/shard_map/dot_general | solution.py:177
  652.0 10.7 fusion.146
  664.4 4.8 convolution_convert_fusion.1
  669.5 7.0 convolution_convert_fusion
  681.5 4.6 fusion.104
  690.3 2.8 fusion.103
  694.9 6.3 all-to-all-start.1
  701.1 7.1 fusion.147
  708.3 7.4 all-to-all-done.1
  717.9 6.1 fusion.148
  729.5 132.8 %all-reduce.17 = (bf16[768]{0:T(1024)(128)(2,1)S(1)}, bf16[768]{0:T(1024)(128)(2,1)S(1)}, bf16[768]{0:T(1024)(128)(2,1)S(1)}, bf16[768]{0:T(1024)(128)(2,1)S(1)}...) all-reduce(bf16[768]{0:T(1024)(128)(2,1)S(1)} %dynamic-update-slice, ...), channel_id=1, replica_groups=mesh['seq'=4,'fsdp'=32] {'fsdp'}, use_global_device_ids=true, to_apply=%add.9 | all-reduce | flops 10752 | bytes 43008
  862.3 3.8 fusion.78
  866.1 103.5 %reduce-scatter.9.cloned.1.call-done = bf16[24,3072]{1,0:T(8,128)(2,1)} async-done(((bf16[768,3072]{1,0:T(8,128)(2,1)}), bf16[24,3072]{1,0:T(8,128)(2,1)}) %reduce-scatter.9.cloned.1.call-update) | async-done | bytes 147472 | tf_op jit(solution)/shard_map/reduce_scatter | solution.py:301
  969.6 167.3 %reduce-scatter.11.cloned.1.call-done = bf16[96,768]{1,0:T(8,128)(2,1)} async-done(((bf16[3072,768]{1,0:T(8,128)(2,1)}), bf16[96,768]{1,0:T(8,128)(2,1)}) %reduce-scatter.11.cloned.1.call-update) | async-done | bytes 147472 | tf_op jit(solution)/shard_map/reduce_scatter | solution.py:307
  1137.4 3.0 fusion.111
  1140.4 153.6 %reduce-scatter.7.cloned.1.call-done = bf16[24,768]{1,0:T(8,128)(2,1)} async-done(((bf16[768,768]{1,0:T(8,128)(2,1)}), bf16[24,768]{1,0:T(8,128)(2,1)}) %reduce-scatter.7.cloned.1.call-update) | async-done | bytes 36880 | tf_op jit(solution)/shard_map/reduce_scatter | solution.py:295
  1294.1 39.5 %all-reduce.19 = (bf16[24]{0:T(256)(128)(2,1)S(1)}, bf16[24]{0:T(256)(128)(2,1)S(1)}, bf16[24]{0:T(256)(128)(2,1)S(1)}, bf16[24]{0:T(256)(128)(2,1)S(1)}, bf16[7...) all-reduce(bf16[24]{0:T(256)(128)(2,1)S(1)} %dynamic-slice.68, ...), channel_id=1, replica_groups=mesh['seq'=4,'fsdp'=32] {'seq'}, use_global_device_ids=true, to_apply=%region_20.21 | all-reduce | flops 18720 | bytes 74880 | tf_op jit(solution)/shard_map/psum | solution.py:315
  1337.3 22.7 %all-reduce.23.cloned.1.call-done = (bf16[24,2304]{1,0:T(8,128)(2,1)}, bf16[24,3072]{1,0:T(8,128)(2,1)}, bf16[96,768]{1,0:T(8,128)(2,1)}) async-done(((bf16[24,2304]{1,0:T(8,128)(2,1)}, bf16[24,3072]{1,0:T(8,128)(2,1)}, bf16[96,768]{1,0:T(8,128)(2,1)}), (bf16[24,2304]{1,0:T(8,128)(2,1)}, bf16[24,3072]{1,0:T(8,128)(2,1)}, bf16[96,768]{1,0:T(8,128)(2,1)})) %all-reduce.23.cloned.1.call-update) | async-done | bytes 405520 | tf_op jit(solution)/shard_map/psum | solution.py:319
  (344 shorter events, 108.2 us)
Async XLA Ops:
  7.2 156.7 %all-gather.8.cloned.1.call-start = ((), (), s32[]{:S(2)}) async-start(), calls=%async_computation.9 | async-start | bytes 1216512 | tf_op jit(solution)/shard_map/all_gather | solution.py:93
  7.9 296.6 %all-gather.6.cloned.1.call-start = ((), (), s32[]{:S(2)}) async-start(), calls=%async_computation.8 | async-start | bytes 3649536 | tf_op jit(solution)/shard_map/all_gather | solution.py:91
  8.7 623.3 %all-gather.10.cloned.1.call-start = ((), (), s32[]{:S(2)}) async-start(), calls=%async_computation.10 | async-start | bytes 4866048 | tf_op jit(solution)/shard_map/all_gather | solution.py:95
  9.4 642.6 %all-gather.12.cloned.1.call-start = ((), (), s32[]{:S(2)}) async-start(), calls=%async_computation.11 | async-start | bytes 4866048 | tf_op jit(solution)/shard_map/all_gather | solution.py:97
  18.1 149.3 %copy-start.44 = (s32[1,2048]{1,0:T(1,128)}, s32[1,2048]{1,0:T(1,128)S(1)}, u32[]{:S(2)}) copy-start(s32[1,2048]{1,0:T(1,128)S(1)} %all-gather) | copy-start | bytes 24580
  24.9 279.6 %copy-start.66 = (f32[512]{0:T(512)}, f32[512]{0:T(512)S(1)}, u32[]{:S(2)}) copy-start(f32[512]{0:T(512)S(1)} %fusion.120) | copy-start | bytes 6148
  163.6 140.9 %copy-start.71 = (f32[768]{0:T(1024)}, f32[768]{0:T(1024)S(1)}, u32[]{:S(2)}) copy-start(f32[768]{0:T(1024)S(1)} %convert_element_type.226) | copy-start | bytes 9220
  163.8 151.7 %copy-start.46 = (f32[512,8]{0,1:T(8,128)}, f32[512,8]{0,1:T(8,128)S(1)}, u32[]{:S(2)}) copy-start(f32[512,8]{0,1:T(8,128)S(1)} %get-tuple-element.203) | copy-start | bytes 49156
  163.8 151.7 %copy-start.48 = (f32[512,8]{0,1:T(8,128)}, f32[512,8]{0,1:T(8,128)S(1)}, u32[]{:S(2)}) copy-start(f32[512,8]{0,1:T(8,128)S(1)} %get-tuple-element.204) | copy-start | bytes 49156
  163.8 140.7 %copy-start.6 = (bf16[1,512,768]{2,1,0:T(8,128)(2,1)S(1)}, bf16[1,512,768]{2,1,0:T(8,128)(2,1)}, u32[]{:S(2)}) copy-start(bf16[1,512,768]{2,1,0:T(8,128)(2,1)} %param.36) | copy-start | bytes 2359300
  167.4 159.1 %all-to-all-start.2 = ((bf16[512,4,192]{0,2,1:T(8,128)(2,1)}), bf16[512,4,192]{0,2,1:T(8,128)(2,1)}, u32[]{:S(2)}, u32[]{:S(2)}) async-start(bf16[512,4,192]{0,2,1:T(8,128)(2,1)} %bitcast.33), calls=%async_computation.2 | async-start | bytes 1572864 | tf_op jit(solution)/shard_map/all_to_all | solution.py:212
  326.4 25.8 %slice-start.9 = ((s32[1,2048]{1,0:T(1,128)}), s32[1,1024]{1,0:T(1,128)S(1)}, s32[]{:S(2)}) async-start(s32[1,2048]{1,0:T(1,128)} %copy-done.44), calls=%async_computation.26 | async-start | bytes 8192 | tf_op jit(solution)/shard_map/slice | solution.py:151
  326.4 27.1 %copy-start.45 = (s32[1,2048]{1,0:T(1,128)S(1)}, s32[1,2048]{1,0:T(1,128)}, u32[]{:S(2)}) copy-start(s32[1,2048]{1,0:T(1,128)} %copy-done.44) | copy-start | bytes 24580
  326.5 78.5 %all-to-all-start = ((bf16[3,512,768]{1,0,2:T(4,128)(2,1)}), bf16[3,512,768]{1,0,2:T(4,128)(2,1)S(1)}, u32[]{:S(2)}, u32[]{:S(2)}) async-start(bf16[3,512,768]{1,0,2:T(4,128)(2,1)} %copy.92), calls=%async_computation | async-start | bytes 6291456 | tf_op jit(solution)/shard_map/all_to_all | solution.py:134
  351.0 515.1 %reduce-scatter.5.cloned.1.call-start = ((), (), s32[]{:S(2)}) async-start(), calls=%async_computation.12 | async-start | bytes 3649536 | tf_op jit(solution)/shard_map/reduce_scatter | solution.py:289
  439.0 4.8 copy-start.15
  439.0 4.8 copy-start.38
  439.0 4.8 copy-start.42
  446.4 23.5 %copy-start = (f32[3,512,2048]{2,1,0:T(8,128)}, f32[3,512,2048]{2,1,0:T(8,128)S(1)}, u32[]{:S(2)}) copy-start(f32[3,512,2048]{2,1,0:T(8,128)S(1)} %get-tuple-element.211) | copy-start | bytes 37748740
  448.3 5.3 copy-start.64
  448.3 13.5 slice-start.3
  448.4 13.5 slice-start.4
  453.6 19.3 %copy-start.5 = (bf16[3,512,512]{1,2,0:T(8,128)(2,1)}, bf16[3,512,512]{1,2,0:T(8,128)(2,1)S(1)}, u32[]{:S(2)}) copy-start(bf16[3,512,512]{1,2,0:T(8,128)(2,1)S(1)} %multiply_convert_fusion.4) | copy-start | bytes 4718596
  453.6 8.2 slice-start.5
  461.9 8.0 copy-start.27
  480.8 9.4 copy-start.1
  484.7 5.5 copy-start.28
  509.8 4.9 copy-start.12
  631.2 338.3 %reduce-scatter.9.cloned.1.call-start = ((), (), s32[]{:S(2)}) async-start(), calls=%async_computation.14 | async-start | bytes 4866048 | tf_op jit(solution)/shard_map/reduce_scatter | solution.py:301
  652.0 12.5 copy-start.8
  669.2 467.6 %reduce-scatter.11.cloned.1.call-start = ((), (), s32[]{:S(2)}) async-start(), calls=%async_computation.15 | async-start | bytes 4866048 | tf_op jit(solution)/shard_map/reduce_scatter | solution.py:307
  680.4 5.6 slice-start.6
  681.4 4.9 slice-start.8
  681.4 5.0 copy-start.26
  681.4 5.0 copy-start.53
  681.4 5.0 copy-start.61
  681.4 7.4 slice-start
  681.5 7.6 slice-start.1
  694.9 20.8 %all-to-all-start.1 = ((bf16[4,512,192]{1,2,0:T(8,128)(2,1)}), bf16[4,512,192]{1,2,0:T(8,128)(2,1)S(1)}, u32[]{:S(2)}, u32[]{:S(2)}) async-start(bf16[4,512,192]{1,2,0:T(8,128)(2,1)} %copy.101), calls=%async_computation.1 | async-start | bytes 1572864 | tf_op jit(solution)/shard_map/all_to_all | solution.py:173
  701.1 14.5 %copy-start.18 = (bf16[1,512,768]{2,1,0:T(8,128)(2,1)S(1)}, bf16[1,512,768]{2,1,0:T(8,128)(2,1)}, u32[]{:S(2)}) copy-start(bf16[1,512,768]{2,1,0:T(8,128)(2,1)} %param.39) | copy-start | bytes 2359300
  701.1 592.9 %reduce-scatter.7.cloned.1.call-start = ((), (), s32[]{:S(2)}) async-start(), calls=%async_computation.13 | async-start | bytes 1216512 | tf_op jit(solution)/shard_map/reduce_scatter | solution.py:295
  717.5 6.9 copy-start.9
  717.5 642.4 %all-reduce.23.cloned.1.call-start = ((), (), s32[]{:S(2)}) async-start(), calls=%async_computation.16 | async-start | bytes 811008 | tf_op jit(solution)/shard_map/psum | solution.py:319
  717.8 6.1 copy-start.20
  717.8 6.1 copy-start.22
  717.9 6.1 copy-start.24
  717.9 6.5 copy-start.75
  1334.0 31.3 %copy-start.78 = (f32[24]{0:T(128)}, f32[24]{0:T(128)S(1)}, u32[]{:S(2)}) copy-start(f32[24]{0:T(128)S(1)} %convert_element_type.275) | copy-start | bytes 292
  (54 other events, 127.8 us)
Sparse Core Ops, SparseCore 0:
  9.7 134.0 all-gather.7
  145.4 159.0 all-gather.5
  306.2 166.1 all-gather.9
  473.8 163.6 all-gather.11
  639.7 158.7 reduce-scatter.4
  800.9 168.5 reduce-scatter.8
  972.1 164.7 reduce-scatter.10
  1139.3 154.6 reduce-scatter.6
  1296.8 63.0 all-reduce.22
where the time goes:
time: 1380 us; the launch traced here: 1370 us
  waiting for transfers between devices  610 us (44%)
  blocking collectives  389 us (28%)
  matrix products  144 us (10%)
  local copies, waits for them, and re-layouts  78.1 us (6%)
  other arithmetic  70.2 us (5%)
  starting transfers between devices  62.3 us (5%)
  between operations  19.6 us (1%)
    unnamed x2, blocking collectives  266 us
    reduce_scatter x1, waiting for transfers between devices, body(): lax.psum_scatter(down_weight_grad.astype(jnp.bfloat16), 'fsdp', scatter_d...  167 us
    reduce_scatter x1, waiting for transfers between devices, body(): lax.psum_scatter(output_weight_grad.astype(jnp.bfloat16), 'fsdp', scatter...  154 us
    all_gather x1, waiting for transfers between devices, body(): lax.all_gather(joint_weight, 'fsdp', axis=0, tiled=True)  107 us
    reduce_scatter x1, waiting for transfers between devices, body(): lax.psum_scatter(up_weight_grad.astype(jnp.bfloat16), 'fsdp', scatter_dim...  103 us
    all_to_all x1, blocking collectives, body(): lax.all_to_all(head_grads, 'seq', split_axis=1, concat_axis=2, tiled=True)  74.8 us
    all_to_all x1, waiting for transfers between devices, body(): lax.all_to_all(stacked, 'seq', split_axis=2, concat_axis=1, tiled=True)  45.8 us
    psum x1, blocking collectives, body(): lax.psum(shares[0].astype(jnp.bfloat16), 'seq').astype(jnp.float32)  39.5 us
  transfers between devices with their start and end apart: 12, of which 7 were waited for; matrix products, arithmetic and copies ran while one was open for 20% of the time, Pallas kernels for 0%

commit v1 on v0

v1 whole, which is shorter than its diff:
```python
import functools
import jax
import jax.numpy as jnp
from jax import lax
from jax.sharding import PartitionSpec as P
from jax.experimental import pallas as pl
from jax.experimental.pallas import tpu as pltpu

MESH = pl.DeviceIdType.MESH


class Place:
    def __init__(self):
        self.seq = lax.axis_index("seq")
        self.fs = lax.axis_index("fsdp")
        self.core = lax.rem(self.seq, 2)
        self.hi = self.seq // 2
        z, xl, y = self.fs // 8, lax.rem(self.fs // 4, 2), lax.rem(self.fs, 4)
        c = self.core
        self.xl = xl
        self.pa, self.pb = y * (1 - c) + z * c, z * (1 - c) + y * c
        self.sa, self.sb = 1 + 7 * c, 8 - 7 * c

    def shard(self, da, dx, db):
        return (
            lax.rem(self.pa + da, 4) * self.sa
            + lax.rem(self.xl + dx, 2) * 4
            + lax.rem(self.pb + db, 4) * self.sb
        )

    def device(self, da, dx, db):
        return (self.seq, self.shard(da, dx, db))

    def sibling(self):
        return (self.seq + 1 - 2 * self.core, self.fs)

    def far(self, dx):
        return (self.seq + 2 - 4 * self.hi, self.shard(0, dx, 0))


def gather_partners(me):
    return [
        me.sibling(),
        me.device(0, 1, 0),
        me.device(1, 0, 0),
        me.device(3, 0, 0),
        me.device(0, 0, 1),
        me.device(0, 0, 3),
    ]


def enter(partners):
    barrier = pltpu.get_barrier_semaphore()
    for partner in partners:
        pl.semaphore_signal(barrier, inc=1, device_id=partner, device_id_type=MESH)
    pl.semaphore_wait(barrier, len(partners))


class Gather:
    def __init__(self, me, src, dst, send, recv, local):
        self.me, self.src, self.dst = me, src, dst
        self.send, self.recv, self.local = send, recv, local
        self.half = dst.shape[2] // 2
        self.sent = []
        self.cols = pl.ds(pl.multiple_of(me.core * self.half, 128), self.half)
        self.other = pl.ds(pl.multiple_of((1 - me.core) * self.half, 128), self.half)

    def slot(self, piece, cols=None):
        return self.dst.at[self.me.shard(*piece), :, self.cols if cols is None else cols]

    def key(self, piece):
        return piece[0] * 8 + piece[1] * 4 + piece[2]

    def push(self, piece, device, lands):
        own = piece == (0, 0, 0)
        src = self.src.at[:, self.cols] if own else self.slot(piece)
        copy = pltpu.make_async_remote_copy(
            src_ref=src,
            dst_ref=self.slot(piece),
            send_sem=self.send.at[len(self.sent)],
            recv_sem=self.recv.at[lands],
            device_id=device,
            device_id_type=MESH,
        )
        copy.start()
        self.sent.append(copy)

    def arrived(self, piece):
        ref = self.slot(piece)
        pltpu.make_async_copy(ref, ref, self.recv.at[self.key(piece)]).wait()
        self.push(piece, self.me.sibling(), 32 + self.key(piece))

    def ring_a(self, piece, step):
        da, dx, db = piece
        to = ((da - step) % 4, dx, db)
        self.push(piece, self.me.device(step % 4, 0, 0), self.key(to))

    def ring_b(self, piece, step):
        da, dx, db = piece
        to = (da, dx, (db - step) % 4)
        self.push(piece, self.me.device(0, 0, step % 4), self.key(to))

    def begin(self):
        self.keep = pltpu.make_async_copy(self.src, self.dst.at[self.me.fs], self.local)
        self.keep.start()
        self.push((0, 0, 0), self.me.device(0, 1, 0), self.key((0, 1, 0)))
        self.ring_a((0, 0, 0), 1)
        self.ring_a((0, 0, 0), -1)
        self.ring_b((0, 0, 0), 1)
        self.ring_b((0, 0, 0), -1)

    def spread_a(self):
        self.arrived((0, 1, 0))
        self.ring_a((0, 1, 0), 1)
        self.ring_a((0, 1, 0), -1)
        self.ring_b((0, 1, 0), 1)
        self.ring_b((0, 1, 0), -1)
        self.arrived((3, 0, 0))
        self.ring_a((3, 0, 0), 1)
        self.arrived((1, 0, 0))
        self.arrived((1, 1, 0))
        self.ring_a((1, 1, 0), -1)
        self.arrived((3, 1, 0))

    def spread_b(self):
        for da in (3, 1):
            for dx in range(2):
                self.ring_b((da, dx, 0), 1)
                self.ring_b((da, dx, 0), -1)
        for dx in range(2):
            self.arrived((2, dx, 0))
            self.ring_b((2, dx, 0), 1)
            self.ring_b((2, dx, 0), -1)

    def finish_b(self):
        for da in (0, 3, 1, 2):
            self.arrived((da, 0, 3))
            self.ring_b((da, 0, 3), 1)
            self.arrived((da, 1, 1))
            self.ring_b((da, 1, 1), -1)
            self.arrived((da, 0, 1))
            self.arrived((da, 1, 3))

    def last_b(self):
        for da in (0, 3, 1, 2):
            self.arrived((da, 0, 2))
            self.arrived((da, 1, 2))

    def end(self):
        for da in range(4):
            for dx in range(2):
                for db in range(4):
                    if (da, dx, db) != (0, 0, 0):
                        ref = self.slot((da, dx, db), self.other)
                        pltpu.make_async_copy(ref, ref, self.recv.at[32 + db * 8 + dx * 4 + da]).wait()
        self.keep.wait()
        for copy in self.sent:
            copy.wait_send()


def gather_kernel(*refs):
    n = 3
    srcs, dsts, (send, recv, local) = refs[:n], refs[n : 2 * n], refs[2 * n :]
    me = Place()
    groups = [Gather(me, srcs[g], dsts[g], send.at[g], recv.at[g], local.at[g]) for g in range(n)]
    enter(gather_partners(me))
    a, b, c = groups
    a.begin()
    a.spread_a()
    b.begin()
    a.spread_b()
    b.spread_a()
    a.finish_b()
    c.begin()
    b.spread_b()
    c.spread_a()
    a.last_b()
    b.finish_b()
    c.spread_b()
    b.last_b()
    c.finish_b()
    c.last_b()
    for group in groups:
        group.end()


def gather_weights(*packs):
    return pl.pallas_call(
        gather_kernel,
        out_shape=[jax.ShapeDtypeStruct((32,) + p.shape, p.dtype) for p in packs],
        in_specs=[pl.BlockSpec(memory_space=pl.ANY)] * len(packs),
        out_specs=[pl.BlockSpec(memory_space=pl.ANY)] * len(packs),
        scratch_shapes=[
            pltpu.SemaphoreType.DMA((len(packs), 64)),
            pltpu.SemaphoreType.DMA((len(packs), 64)),
            pltpu.SemaphoreType.DMA((len(packs),)),
        ],
        compiler_params=pltpu.CompilerParams(collective_id=1, has_side_effects=True),
        name="gather_weights",
    )(*packs)


def total_partners(me):
    return gather_partners(me) + [me.far(0), me.far(1)]


class Total:
    def __init__(self, me, part, out, acc, sib, inbox, mine, theirs, send, recv, local):
        self.me, self.part, self.out = me, part, out
        self.acc, self.sib, self.inbox, self.mine, self.theirs = acc, sib, inbox, mine, theirs
        self.send, self.recv, self.local = send, recv, local
        self.half = part.shape[2] // 2
        self.cols = pl.ds(pl.multiple_of(me.core * self.half, 128), self.half)
        self.other = pl.ds(pl.multiple_of((1 - me.core) * self.half, 128), self.half)
        self.sent = []

    def key(self, da, dx, db):
        return (da % 4) * 8 + dx * 4 + db % 4

    def push(self, src, dst, device, lands):
        copy = pltpu.make_async_remote_copy(
            src_ref=src,
            dst_ref=dst,
            send_sem=self.send.at[len(self.sent)],
            recv_sem=self.recv.at[lands],
            device_id=device,
            device_id_type=MESH,
        )
        copy.start()
        self.sent.append(copy)

    def arrived(self, ref, lands):
        pltpu.make_async_copy(ref, ref, self.recv.at[lands]).wait()

    def begin(self):
        self.loads = {}
        for da, dx, db in self.order():
            k = self.key(da, dx, db)
            self.push(
                self.part.at[self.me.shard(db, dx, da), :, self.other],
                self.sib.at[k],
                self.me.sibling(),
                k,
            )
            load = pltpu.make_async_copy(
                self.part.at[self.me.shard(da, dx, db), :, self.cols], self.acc.at[k], self.local.at[k]
            )
            load.start()
            self.loads[k] = load

    def order(self):
        return [(da, dx, db) for db in (2, 1, 3, 0) for da in (2, 1, 3, 0) for dx in range(2)]

    def add(self, k, ref):
        self.acc[k] = (self.acc[k].astype(jnp.float32) + ref[...].astype(jnp.float32)).astype(jnp.bfloat16)

    def add_sib(self, da, dx, db):
        k = self.key(da, dx, db)
        self.loads[k].wait()
        self.arrived(self.sib.at[k], k)
        self.add(k, self.sib.at[k])

    def hop(self, piece, device, slot):
        self.push(self.acc.at[self.key(*piece)], self.inbox.at[slot], device, 32 + slot)

    def take(self, piece, slot):
        self.arrived(self.inbox.at[slot], 32 + slot)
        self.add(self.key(*piece), self.inbox.at[slot])

    def first_b(self):
        me = self.me
        up, down = me.device(0, 0, 1), me.device(0, 0, 3)
        for da in (2, 1, 3, 0):
            self.add_sib(da, 0, 2)
            self.hop((da, 0, 2), up, da * 2)
            self.add_sib(da, 1, 2)
            self.hop((da, 1, 2), down, da * 2 + 1)
        for da in (2, 1, 3, 0):
            self.add_sib(da, 1, 1)
            self.hop((da, 1, 1), up, 8 + da * 4 + 2)
            self.add_sib(da, 0, 3)
            self.hop((da, 0, 3), down, 8 + da * 4 + 1)
        for da in (2, 1, 3, 0):
            self.add_sib(da, 0, 1)
            self.add_sib(da, 1, 3)

    def second_b(self):
        me = self.me
        up, down = me.device(0, 0, 1), me.device(0, 0, 3)
        for da in (2, 1, 3, 0):
            self.take((da, 0, 1), da * 2)
            self.hop((da, 0, 1), up, 8 + da * 4)
            self.take((da, 1, 3), da * 2 + 1)
            self.hop((da, 1, 3), down, 8 + da * 4 + 3)
        for da in (2, 1, 3, 0):
            for dx in range(2):
                self.add_sib(da, dx, 0)

    def first_a(self):
        me = self.me
        up, down = me.device(1, 0, 0), me.device(3, 0, 0)
        for da in (2, 1, 3, 0):
            for dx in range(2):
                for side in range(2):
                    self.take((da, dx, 0), 8 + da * 4 + dx * 2 + side)
            if da == 2:
                self.hop((2, 0, 0), up, 24)
                self.hop((2, 1, 0), down, 25)
            if da == 1:
                self.hop((1, 1, 0), up, 28)
            if da == 3:
                self.hop((3, 0, 0), down, 27)

    def second_a(self):
        me = self.me
        self.take((1, 0, 0), 24)
        self.hop((1, 0, 0), me.device(1, 0, 0), 26)
        self.take((3, 1, 0), 25)
        self.hop((3, 1, 0), me.device(3, 0, 0), 29)

    def along_x(self):
        me = self.me
        for dx in (1, 0):
            for side in range(2):
                self.take((0, dx, 0), 26 + dx * 2 + side)
            if dx == 1:
                self.hop((0, 1, 0), me.device(0, 1, 0), 30)
                self.hop((0, 1, 0), me.far(1), 31)
        self.hop((0, 0, 0), me.far(0), 32)

    def total(self):
        for slot in (30, 31, 32):
            self.arrived(self.inbox.at[slot], 32 + slot)
        wide = lambda ref: ref[...].astype(jnp.float32)
        own = wide(self.acc.at[0]) + wide(self.inbox.at[32])
        near = wide(self.inbox.at[30]) + wide(self.inbox.at[31])
        done = (own + near).astype(jnp.bfloat16)
        self.mine[...] = done
        self.push(self.mine, self.theirs, self.me.sibling(), 65)
        self.out[:, self.cols] = done.astype(jnp.float32)

    def end(self):
        self.arrived(self.theirs, 65)
        self.out[:, self.other] = self.theirs[...].astype(jnp.float32)
        for copy in self.sent:
            copy.wait_send()


def total_scratch(shape):
    rows, half = shape[1], shape[2] // 2
    return [
        pltpu.VMEM((32, rows, half), jnp.bfloat16),
        pltpu.VMEM((32, rows, half), jnp.bfloat16),
        pltpu.VMEM((33, rows, half), jnp.bfloat16),
        pltpu.VMEM((rows, half), jnp.bfloat16),
        pltpu.VMEM((rows, half), jnp.bfloat16),
        pltpu.SemaphoreType.DMA((80,)),
        pltpu.SemaphoreType.DMA((66,)),
        pltpu.SemaphoreType.DMA((32,)),
    ]


def run_totals(groups):
    n = len(groups)
    stages = ["first_b", "second_b", "first_a", "second_a", "along_x", "total"]
    for tick in range(len(stages) + 2 * (n - 1)):
        for g in range(n):
            s = tick - 2 * g
            if 0 <= s < len(stages):
                getattr(groups[g], stages[s])()
    for group in groups:
        group.end()


def total_kernel(n, *refs):
    parts, outs, scratch = refs[:n], refs[n : 2 * n], refs[2 * n :]
    me = Place()
    groups = [Total(me, parts[g], outs[g], *scratch[8 * g : 8 * g + 8]) for g in range(n)]
    enter(total_partners(me))
    for group in groups:
        group.begin()
    run_totals(groups)


def sum_grads(*parts):
    scratch = []
    for p in parts:
        scratch += total_scratch(p.shape)
    return pl.pallas_call(
        functools.partial(total_kernel, len(parts)),
        out_shape=[jax.ShapeDtypeStruct(p.shape[1:], jnp.float32) for p in parts],
        in_specs=[pl.BlockSpec(memory_space=pl.ANY)] * len(parts),
        out_specs=[pl.BlockSpec(memory_space=pltpu.VMEM)] * len(parts),
        scratch_shapes=scratch,
        compiler_params=pltpu.CompilerParams(
            collective_id=2, has_side_effects=True, vmem_limit_bytes=56 << 20
        ),
        name="sum_grads",
    )(*parts)


def exchange_kernel(src, dst, send, recv, local):
    seq, fs = lax.axis_index("seq"), lax.axis_index("fsdp")
    enter([(lax.rem(seq + k, 4), fs) for k in (1, 2, 3)])
    keep = pltpu.make_async_copy(src.at[seq], dst.at[seq], local)
    keep.start()
    copies = []
    for k in (2, 1, 3):
        to = lax.rem(seq + k, 4)
        copy = pltpu.make_async_remote_copy(
            src_ref=src.at[to],
            dst_ref=dst.at[seq],
            send_sem=send.at[k - 1],
            recv_sem=recv.at[k - 1],
            device_id=(to, fs),
            device_id_type=MESH,
        )
        copy.start()
        copies.append(copy)
    keep.wait()
    for copy in copies:
        copy.wait()


def exchange(x, channel):
    return pl.pallas_call(
        exchange_kernel,
        out_shape=jax.ShapeDtypeStruct(x.shape, x.dtype),
        in_specs=[pl.BlockSpec(memory_space=pl.ANY)],
        out_specs=pl.BlockSpec(memory_space=pl.ANY),
        scratch_shapes=[pltpu.SemaphoreType.DMA((3,)), pltpu.SemaphoreType.DMA((3,)), pltpu.SemaphoreType.DMA],
        compiler_params=pltpu.CompilerParams(collective_id=channel, has_side_effects=True),
        name="exchange",
    )(x)


BLK = 512
F32, BF16 = jnp.float32, jnp.bfloat16


def dot(a, b):
    return jnp.dot(a, b, preferred_element_type=F32)


def split_heads(x_ref, rows, s):
    q, qt, k, kt, v, vt, g, gt = s
    sl = pl.ds(rows * BLK, BLK)
    x = x_ref[rows]
    for h in range(3):
        for a, (r, t) in enumerate(((q, qt), (k, kt), (v, vt), (g, gt))):
            part = x[:, a * 192 + h * 64 : a * 192 + h * 64 + 64]
            if a == 0:
                part = part * jnp.asarray(0.125, BF16)
            r[h, sl, :] = part
            t[h, :, sl] = part.T


def masked(scores, i, j, doc_row, doc_col):
    if i == j:
        key = lax.broadcasted_iota(jnp.int32, (BLK, BLK), 0)
        query = lax.broadcasted_iota(jnp.int32, (BLK, BLK), 1)
        allowed = key <= query
        if i in (0, 3):
            allowed = allowed & (doc_col[pl.ds(j * BLK, BLK), :] == doc_row[:, pl.ds(i * BLK, BLK)])
        return jnp.where(allowed, scores, -1e30)
    if i == 3 or j == 0:
        allowed = doc_col[pl.ds(j * BLK, BLK), :] == doc_row[:, pl.ds(i * BLK, BLK)]
        return jnp.where(allowed, scores, -1e30)
    return scores


def attend_block(h, i, s, doc_row, doc_col, score, expo, dk, dv, out):
    q, qt, k, kt, v, vt, g, gt = s
    me = pl.ds(i * BLK, BLK)
    q_i, qt_i, gt_i = q[h, me, :], qt[h, :, me], gt[h, :, me]
    peak = None
    for j in range(i + 1):
        rows = pl.ds(j * BLK, BLK)
        sc = masked(dot(k[h, rows, :], qt_i), i, j, doc_row, doc_col)
        score[rows, :] = sc
        top = jnp.max(sc, axis=0, keepdims=True)
        peak = top if peak is None else jnp.maximum(peak, top)
    total, ctx = 0.0, 0.0
    for j in range(i + 1):
        rows = pl.ds(j * BLK, BLK)
        e = jnp.exp(score[rows, :] - peak)
        total = total + jnp.sum(e, axis=0, keepdims=True)
        e = e.astype(BF16)
        expo[rows, :] = e
        ctx = ctx + dot(vt[h, :, rows], e)
    inverse = 1.0 / total
    ctx = ctx * inverse
    gt_wide = gt_i.astype(F32)
    weighted = jnp.sum(ctx * gt_wide, axis=0, keepdims=True) * inverse
    scaled = (gt_wide * inverse).astype(BF16)
    scaled_rows = scaled.T
    dq = 0.0
    for j in range(i, -1, -1):
        rows = pl.ds(j * BLK, BLK)
        e = expo[rows, :]
        dp = dot(v[h, rows, :], scaled)
        ds = (e.astype(F32) * (dp - weighted)).astype(BF16)
        add_v, add_k = dot(e, scaled_rows), dot(ds, q_i)
        if i == 3:
            dv[h, rows, :], dk[h, rows, :] = add_v, add_k
        else:
            dv[h, rows, :] += add_v
            dk[h, rows, :] += add_k
        dq = dq + dot(kt[h, :, rows], ds)
    out[h, 0] = ctx.T.astype(BF16)
    out[h, 1] = (dq * 0.125).T.astype(BF16)


def join_heads(i, out, dk, dv, y_ref):
    me = pl.ds(i * BLK, BLK)
    parts = [out[h, 0] for h in range(3)] + [out[h, 1] for h in range(3)]
    parts += [dk[h, me, :].astype(BF16) for h in range(3)] + [dv[h, me, :].astype(BF16) for h in range(3)]
    y_ref[i] = jnp.concatenate(parts, axis=1)


def attn_scratch():
    rows, cols = pltpu.VMEM((3, 2048, 64), BF16), pltpu.VMEM((3, 64, 2048), BF16)
    return [rows, cols] * 4 + [
        pltpu.VMEM((2048, BLK), F32),
        pltpu.VMEM((2048, BLK), BF16),
        pltpu.VMEM((3, 2048, 64), F32),
        pltpu.VMEM((3, 2048, 64), F32),
        pltpu.VMEM((3, 2, BLK, 64), BF16),
    ]


def attn_kernel(x_ref, doc_row, doc_col, y_ref, *scr):
    s, (score, expo, dk, dv, out) = scr[:8], scr[8:]
    for b in range(4):
        split_heads(x_ref, b, s)
    for i in (3, 2, 1, 0):
        def head(h, c):
            attend_block(h, i, s, doc_row, doc_col, score, expo, dk, dv, out)
            return c
        lax.fori_loop(0, 3, head, 0)
        join_heads(i, out, dk, dv, y_ref)


def attention(x, labels):
    return pl.pallas_call(
        attn_kernel,
        out_shape=jax.ShapeDtypeStruct((4, BLK, 768), BF16),
        in_specs=[pl.BlockSpec(memory_space=pltpu.VMEM)] * 3,
        out_specs=pl.BlockSpec(memory_space=pltpu.VMEM),
        scratch_shapes=attn_scratch(),
        compiler_params=pltpu.CompilerParams(vmem_limit_bytes=56 << 20),
        name="attention",
    )(x, labels.reshape(1, 2048), labels.reshape(2048, 1))


HEADS = 12
HEAD_DIM = 64
ROT = 16


def gelu_exact(values):
    return jax.nn.gelu(values, approximate=False)


def rotary_tables(places):
    freqs = 10000.0 ** (-jnp.arange(0, ROT, 2).astype(jnp.float32) / ROT)
    turned = places.astype(jnp.float32)[:, None] * freqs[None, :]
    cosine, sine = jnp.cos(turned), jnp.sin(turned)
    rest = places.shape[0], HEAD_DIM - ROT
    none = jnp.zeros_like(sine)
    wide = lambda parts: jnp.tile(jnp.concatenate(parts, axis=1), (1, 3))
    return (
        wide([cosine, cosine, jnp.ones(rest, jnp.float32)]),
        wide([sine, none, jnp.zeros(rest, jnp.float32)]),
        wide([none, sine, jnp.zeros(rest, jnp.float32)]),
    )


def rotate(x, tables, sign):
    cosine, low, high = tables
    return (
        x * cosine
        - sign * jnp.roll(x, -8, axis=-1) * low
        + sign * jnp.roll(x, 8, axis=-1) * high
    )


def by_group(w):
    return w.reshape(w.shape[:-1] + (3, 4, 192)).swapaxes(-3, -2).reshape(w.shape)


def by_array(w):
    return w.reshape(w.shape[:-1] + (4, 3, 192)).swapaxes(-3, -2).reshape(w.shape)


def body(
    hidden_states,
    positions,
    documents,
    cotangent,
    first_gain,
    first_shift,
    second_gain,
    second_shift,
    joint_weight,
    joint_bias,
    output_weight,
    output_bias,
    up_weight,
    up_bias,
    down_weight,
    down_bias,
):
    small = jnp.concatenate(
        [v[:, None] for v in (first_gain, first_shift, second_gain, second_shift, output_bias, down_bias)]
        + [joint_bias.reshape(24, 3), up_bias.reshape(24, 4), jnp.zeros((24, 243), BF16)],
        axis=1,
    )
    pack = jnp.concatenate([by_group(joint_weight), output_weight, small], axis=1)
    pack_all, up_all, down_all = gather_weights(pack, up_weight, down_weight)
    pack_all = pack_all.reshape(768, 3328)
    up_full, down_full = up_all.reshape(768, 3072), down_all.reshape(3072, 768)
    joint_full, output_full = pack_all[:, :2304], pack_all[:, 2304:3072]
    vectors = pack_all[:, 3072:3200].astype(jnp.float32)
    gain_one, shift_one, gain_two, shift_two, output_shift, down_shift = (vectors[:, i] for i in range(6))
    joint_shift = by_group(vectors[:, 6:9].reshape(2304))
    up_shift = vectors[:, 9:13].reshape(3072)

    states = hidden_states[0].astype(jnp.float32)
    average = jnp.mean(states, axis=-1, keepdims=True)
    centered = states - average
    root = lax.rsqrt(jnp.mean(centered * centered, axis=-1, keepdims=True) + 1e-05)
    xhat = centered * root
    first_in = (xhat * gain_one + shift_one).astype(BF16)
    second_in = (xhat * gain_two + shift_two).astype(BF16)
    tangent = cotangent[0]
    tables = rotary_tables(positions[0])
    projected = (jnp.dot(first_in, joint_full, preferred_element_type=F32) + joint_shift).reshape(512, 4, 3, 192)
    wide_tables = tuple(t[:, None, :] for t in tables)
    context_grad = lax.dot_general(tangent, output_full, (((1,), (1,)), ((), ())), preferred_element_type=F32)
    to_heads = jnp.concatenate(
        [
            rotate(projected[:, :, 0], wide_tables, 1.0).astype(BF16),
            rotate(projected[:, :, 1], wide_tables, 1.0).astype(BF16),
            projected[:, :, 2].astype(BF16),
            context_grad.reshape(512, 4, 192).astype(BF16),
        ],
        axis=2,
    ).swapaxes(0, 1)
    labels = lax.all_gather(documents[0], "seq", axis=0, tiled=True)
    by_heads = exchange(to_heads, 3)
    by_tokens = exchange(attention(by_heads, labels), 4)
    by_tokens = by_tokens.swapaxes(0, 1)
    context = by_tokens[:, :, :192].reshape(512, 768)
    attn_out = jnp.dot(context, output_full, preferred_element_type=F32) + output_shift
    hidden_pre = jnp.dot(second_in, up_full, preferred_element_type=F32) + up_shift
    activated, gelu_pull = jax.vjp(gelu_exact, hidden_pre)
    act_low = activated.astype(BF16)
    mlp_out = jnp.dot(act_low, down_full, preferred_element_type=F32) + down_shift
    layer_output = (states + attn_out + mlp_out).astype(BF16)

    tangent_wide = tangent.astype(F32)
    bias_sum = jnp.sum(tangent_wide, axis=0)
    down_weight_grad = jnp.einsum("tf,td->fd", act_low, tangent, preferred_element_type=F32)
    act_grad = jnp.einsum("td,fd->tf", tangent, down_full, preferred_element_type=F32)
    hidden_grad = gelu_pull(act_grad)[0].astype(BF16)
    up_weight_grad = jnp.einsum("td,tf->df", second_in, hidden_grad, preferred_element_type=F32)
    up_bias_grad = jnp.sum(hidden_grad.astype(F32), axis=0)
    second_grad = jnp.einsum("tf,df->td", hidden_grad, up_full, preferred_element_type=F32)
    output_weight_grad = jnp.einsum("td,te->de", context, tangent, preferred_element_type=F32)
    wide = by_tokens.astype(F32)
    joint_grad = jnp.concatenate(
        [
            rotate(wide[:, :, 192:384], wide_tables, -1.0),
            rotate(wide[:, :, 384:576], wide_tables, -1.0),
            wide[:, :, 576:],
        ],
        axis=2,
    ).astype(BF16).reshape(512, 2304)
    joint_weight_grad = jnp.einsum("td,tc->dc", first_in, joint_grad, preferred_element_type=F32)
    joint_bias_grad = by_array(jnp.sum(joint_grad.astype(F32), axis=0))
    first_grad = jnp.einsum("tc,dc->td", joint_grad, joint_full, preferred_element_type=F32)

    def norm_back(grad, gain):
        scaled = grad * gain
        mean_one = jnp.mean(scaled, axis=-1, keepdims=True)
        mean_two = jnp.mean(scaled * xhat, axis=-1, keepdims=True)
        return root * (scaled - mean_one - xhat * mean_two)

    input_grad = (tangent_wide + norm_back(first_grad, gain_one) + norm_back(second_grad, gain_two)).astype(BF16)
    sums = [
        jnp.sum(first_grad * xhat, axis=0),
        jnp.sum(first_grad, axis=0),
        jnp.sum(second_grad * xhat, axis=0),
        jnp.sum(second_grad, axis=0),
        bias_sum,
        bias_sum,
    ]
    small_grad = jnp.concatenate(
        [v[:, None] for v in sums]
        + [joint_bias_grad.reshape(768, 3), up_bias_grad.reshape(768, 4), jnp.zeros((768, 243), F32)],
        axis=1,
    )
    pack_grad = jnp.concatenate(
        [joint_weight_grad.astype(BF16), output_weight_grad.astype(BF16), small_grad.astype(BF16)], axis=1
    )
    pack_sum, up_sum, down_sum = sum_grads(
        pack_grad.reshape(32, 24, 3328),
        up_weight_grad.astype(BF16).reshape(32, 24, 3072),
        down_weight_grad.astype(BF16).reshape(32, 96, 768),
    )
    vector_sums = pack_sum[:, 3072:3200]
    return (
        layer_output[None],
        input_grad[None],
        vector_sums[:, 0],
        vector_sums[:, 1],
        vector_sums[:, 2],
        vector_sums[:, 3],
        by_array(pack_sum[:, :2304]),
        vector_sums[:, 6:9].reshape(72),
        pack_sum[:, 2304:3072],
        vector_sums[:, 4],
        up_sum,
        vector_sums[:, 9:13].reshape(96),
        down_sum,
        vector_sums[:, 5],
    )


def solution(mesh):
    in_specs = (
        P("fsdp", "seq", None),
        P("fsdp", "seq"),
        P("fsdp", "seq"),
        P("fsdp", "seq", None),
        P("fsdp"),
        P("fsdp"),
        P("fsdp"),
        P("fsdp"),
        P("fsdp", None),
        P("fsdp"),
        P("fsdp", None),
        P("fsdp"),
        P("fsdp", None),
        P("fsdp"),
        P("fsdp", None),
        P("fsdp"),
    )
    out_specs = (
        P("fsdp", "seq", None),
        P("fsdp", "seq", None),
        P("fsdp"),
        P("fsdp"),
        P("fsdp"),
        P("fsdp"),
        P("fsdp", None),
        P("fsdp"),
        P("fsdp", None),
        P("fsdp"),
        P("fsdp", None),
        P("fsdp"),
        P("fsdp", None),
        P("fsdp"),
    )
    return jax.shard_map(body, mesh=mesh, in_specs=in_specs, out_specs=out_specs, check_vma=False)
```

time: 1380 us -> 411 us (0.30)
  waiting for transfers between devices: 610 us -> 0 us
  blocking collectives: 389 us -> 8.01 us
  Pallas kernels: 0 us -> 229 us
  matrix products: 144 us -> 68.5 us
  starting transfers between devices: 62.3 us -> 0 us
  other arithmetic: 70.2 us -> 20.3 us
  between operations: 19.6 us -> 1.78 us
    reduce_scatter x4 -> x0, waiting for transfers between devices: 424 us -> none  [the longest x1 167 us: body(): lax.psum_scatter(down_weight_grad.astype(jnp.bfloat16), 'fsdp', scatter_d...]
    unnamed x2 -> x0, blocking collectives: 266 us -> none
    pallas_call x0 -> x5, Pallas kernels: none -> 229 us  [the longest x2 76.2 us: exchange(): pl.pallas_call(exchange_kernel, out_shape=jax.ShapeDtypeStruct(x.shape, x...]
    all_gather x4 -> x0, waiting for transfers between devices: 107 us -> none  [the longest x1 107 us: body(): lax.all_gather(joint_weight, 'fsdp', axis=0, tiled=True)]
    dot_general x36 -> x12, matrix products: 144 us -> 68.5 us  [the longest x1 19.6 us: body(): jnp.dot(second_in, up_full, preferred_element_type=F32) + up_shift]
    all_to_all x1 -> x0, blocking collectives: 74.8 us -> none  [body(): lax.all_to_all(head_grads, 'seq', split_axis=1, concat_axis=2, tiled=True)]
    all_to_all x3 -> x0, starting transfers between devices: 61.3 us -> none  [the longest x1 30.5 us: body(): lax.all_to_all(context_grad, 'seq', split_axis=1, concat_axis=0, tiled=True)]
    all_to_all x3 -> x0, waiting for transfers between devices: 53.2 us -> none  [the longest x1 45.8 us: body(): lax.all_to_all(stacked, 'seq', split_axis=2, concat_axis=1, tiled=True)]
  transfers between devices with their start and end apart: 12 -> 0, of which waited for: 7 -> 0; matrix products, arithmetic and copies ran while one was open for 20% -> 0% of each run, Pallas kernels for 0% -> 0%
where the time goes in v1:
time: 411 us; the launch traced here: 404 us
  Pallas kernels  229 us (56%)
  local copies, waits for them, and re-layouts  76.4 us (19%)
  matrix products  68.5 us (17%)
  other arithmetic  20.3 us (5%)
  blocking collectives  8.01 us (2%)
    pallas_call x2, Pallas kernels, exchange(): pl.pallas_call(exchange_kernel, out_shape=jax.ShapeDtypeStruct(x.shape, x...  76.2 us
    pallas_call x1, Pallas kernels, sum_grads(): pl.pallas_call(functools.partial(total_kernel, len(parts)), out_shape=[ja...  60.6 us
    pallas_call x1, Pallas kernels, gather_weights(): pl.pallas_call(gather_kernel, out_shape=[jax.ShapeDtypeStruct((32,) + p.s...  54.5 us
    pallas_call x1, Pallas kernels, attention(): pl.pallas_call(attn_kernel, out_shape=jax.ShapeDtypeStruct((4, BLK, 768),...  37.6 us
    dot_general x1, matrix products, body(): jnp.dot(second_in, up_full, preferred_element_type=F32) + up_shift  19.6 us
    concatenate x1, local copies, waits for them, and re-layouts, body(): jnp.concatenate([joint_weight_grad.astype(BF16), output_weight_grad.astyp...  9.19 us
    dot_general x1, matrix products, body(): jnp.einsum('td,fd->tf', tangent, down_full, preferred_element_type=F32)  8.87 us
    slice x4, local copies, waits for them, and re-layouts, rotate(): jnp.roll(x, 8, axis=-1)  8.63 us

profile of v1, /device:TPU:1, one launch (start us, length us, event | category | flops | bytes accessed | tf_op | source)
XLA Modules:
  0.0 403.9 jit_solution(15111763615686380761)
XLA Ops:
  1.5 1.3 reduce.4
  2.8 1.3 convert_reduce_fusion
  4.1 1.5 fusion.53
  11.6 8.0 %all-gather.doc_row = s32[1,2048]{1,0:T(1,128)S(1)} all-gather(s32[1,512]{1,0:T(1,128)} %param.18), channel_id=2, replica_groups=mesh['seq'=4,'fsdp'=32] {'seq'}, dimensions={1}, use_global_device_ids=true | all-gather | bytes 10240 | tf_op jit(solution)/shard_map/all_gather | solution.py:650
  19.8 1.1 reshape.228
  24.5 1.0 copy.126
  26.6 1.4 copy.122.doc_col
  27.9 54.5 %gather_weights.1 = (bf16[32,24,3328]{2,1,0:T(8,128)(2,1)}, bf16[32,24,3072]{2,1,0:T(8,128)(2,1)}, bf16[32,96,768]{2,1,0:T(8,128)(2,1)}) custom-call(bf16[24,3328]{1,0:T(8,128)(2,1)} %concatenate.50.refs_0_, bf16[24,3072]{1,0:T(8,128)(2,1)} %refs_1_.1, bf16[96,768]{1,0:T(8,128)(2,1)} %refs_2_.1), custom_call_target="tpu_custom_call" | custom-call | tf_op jit(solution)/shard_map/gather_weights/pallas_call | solution.py:188
  84.6 3.0 convolution_convert_fusion.4
  87.6 2.4 copy.121
  90.1 6.3 %convolution_add_fusion = f32[512,2304]{1,0:T(8,128)} fusion(bf16[768,3328]{1,0:T(8,128)(2,1)} %bitcast.194, f32[2304]{0:T(1024)S(1)} %add.110, bf16[1,512,768]{2,1,0:T(8,128)(2,1)S(1)} %copy-done.2, f32[768]{0:T(1024)S(1)} %get-tuple-element.42, f32[768]{0:T(1024)S(1)} %get-tuple-element.43, f32[512]{0:T(512)S(1)} %add_rsqrt_fusion, ...), kind=kOutput, calls=%fused_computation.29 | convolution fusion | flops 1815478272 | bytes 9063424 | tf_op jit(solution)/shard_map/dot_general | solution.py:638
  96.4 6.0 %copy.114 = f32[512,2304]{0,1:T(8,128)} copy(f32[512,2304]{1,0:T(8,128)} %convolution_add_fusion) | data formatting | bytes 9437184 | tf_op jit(solution)/shard_map/add | solution.py:638
  102.4 1.5 slice.263
  103.9 3.8 fusion.98
  107.8 1.3 copy.141
  109.1 1.8 copy.139
  110.9 2.9 copy.140
  113.8 2.4 fusion.99
  116.2 1.6 fusion.100
  117.8 3.5 fusion.22
  121.4 3.2 maximum_bitcast_fusion.src
  124.6 38.0 %exchange.2.x_ref = bf16[4,512,768]{2,1,0:T(8,128)(2,1)} custom-call(bf16[4,512,768]{2,1,0:T(8,128)(2,1)} %maximum_bitcast_fusion.src), custom_call_target="tpu_custom_call" | custom-call | tf_op jit(solution)/shard_map/exchange/pallas_call | solution.py:426
  162.7 37.6 %attention.1.src = bf16[4,512,768]{2,1,0:T(8,128)(2,1)} custom-call(bf16[4,512,768]{2,1,0:T(8,128)(2,1)} %exchange.2.x_ref, s32[1,2048]{1,0:T(1,128)} %copy-done.18, s32[2048,1]{1,0:T(8,128)} %copy.122.doc_col), custom_call_target="tpu_custom_call" | custom-call | tf_op jit(solution)/shard_map/attention/pallas_call | solution.py:545
  200.3 38.1 %exchange.3 = bf16[4,512,768]{2,1,0:T(8,128)(2,1)} custom-call(bf16[4,512,768]{2,1,0:T(8,128)(2,1)} %attention.1.src), custom_call_target="tpu_custom_call" | custom-call | tf_op jit(solution)/shard_map/exchange/pallas_call | solution.py:426
  238.4 2.3 slice.215
  240.7 2.5 copy.123
  243.2 3.2 convolution_convert_fusion.3
  246.9 2.9 fusion.96
  249.8 1.8 fusion.97
  251.6 4.8 %fusion.19 = (bf16[512,4,192]{2,0,1:T(8,128)(2,1)S(1)}, bf16[512,4,192]{2,0,1:T(8,128)(2,1)S(1)}, bf16[512,4,192]{2,0,1:T(8,128)(2,1)S(1)}) fusion(f32[512,4,768]{2,0,1:T(8,128)S(1)} %bitcast_convert_fusion, f32[512,4,8]{2,0,1:T(8,128)} %get-tuple-element.60, f32[512,4,184]{2,0,1:T(8,128)S(1)} %get-tuple-element.64, ...), kind=kLoop, calls=%fused_computation.42 | loop fusion | flops 6291456 | bytes 13762560 | tf_op jit(solution)/shard_map/add | solution.py:582
  256.4 1.2 fusion.94
  257.7 1.1 reshape_reshape.8
  258.7 2.6 copy.127
  261.3 6.1 %convolution_convert_fusion.2 = bf16[768,2304]{1,0:T(8,128)(2,1)} fusion(bf16[512,2304]{0,1:T(8,128)(2,1)} %bitcast.178, bf16[1,512,768]{2,1,0:T(8,128)(2,1)S(1)} %copy-done.3, f32[768]{0:T(1024)S(1)} %get-tuple-element.42, f32[768]{0:T(1024)S(1)} %get-tuple-element.43, f32[512]{0:T(512)S(1)} %add_rsqrt_fusion, f32[512]{0:T(512)S(1)} %broadcast_multiply_fusion.4), kind=kOutput, calls=%fused_computation.28 | convolution fusion | flops 1816068096 | bytes 6694912 | tf_op jit(solution)/shard_map/td,tc->dc/dot_general | solution.py:680
  267.4 19.6 %multiply_convert_fusion = (bf16[512,3072]{1,0:T(8,128)(2,1)S(1)}, f32[512,3072]{1,0:T(8,128)}, f32[512,3072]{1,0:T(8,128)}) fusion(f32[3072]{0:T(1024)S(1)} %add.122, bf16[768,3072]{1,0:T(8,128)(2,1)} %bitcast.205, bf16[1,512,768]{2,1,0:T(8,128)(2,1)S(1)} %copy-done.3, f32[768]{0:T(1024)S(1)} %get-tuple-element.40, f32[768]{0:T(1024)S(1)} %get-tuple-element.41, ...), kind=kOutput, calls=%fused_computation.11 | convolution fusion | flops 2522087424 | bytes 21256192 | tf_op jit(solution)/shard_map/dot_general | solution.py:656
  287.0 8.9 %fusion.103 = (bf16[3072]{0:T(1024)(128)(2,1)S(1)}, bf16[512,3072]{1,0:T(8,128)(2,1)S(1)}) fusion(f32[512,3072]{1,0:T(8,128)} %get-tuple-element.53, bf16[3072,768]{1,0:T(8,128)(2,1)S(1)} %bitcast.211, bf16[1,512,768]{2,1,0:T(8,128)(2,1)S(1)} %copy-done.9, f32[512,3072]{1,0:T(8,128)} %get-tuple-element.81, f32[3072]{0:T(1024)S(1)} %add.122), kind=kOutput, calls=%fused_computation.162 | convolution fusion | flops 2441081856 | bytes 21252096 | tf_op jit(solution)/shard_map/td,fd->tf/dot_general | solution.py:665
  295.9 2.6 fusion.104
  298.6 1.8 fusion.63
  300.4 2.6 fusion.105
  303.1 3.1 fusion.49
  306.3 1.9 fusion.93
  308.2 1.1 reshape.240
  312.7 9.2 %concatenate.64 = bf16[768,3328]{1,0:T(8,128)(2,1)} concatenate(bf16[768,2304]{1,0:T(8,128)(2,1)} %convolution_convert_fusion.2, bf16[768,768]{1,0:T(8,128)(2,1)S(1)} %copy-done.13, bf16[768,1]{1,0:T(8,128)(2,1)} %broadcast_in_dim.81, bf16[768,1]{1,0:T(8,128)(2,1)} %broadcast_in_dim.82, bf16[768,1]{1,0:T(8,128)(2,1)} %broadcast_in_dim.83, bf16[768,1]{1,0:T(8,128)(2,1)} %broadcast_in_dim.84, ...), dimensions={1} | concatenate | bytes 10223616 | tf_op jit(solution)/shard_map/concatenate | solution.py:704
  321.9 6.7 %convolution_convert_fusion.1 = bf16[768,3072]{1,0:T(8,128)(2,1)} fusion(bf16[512,3072]{1,0:T(8,128)(2,1)} %copy-done.24, bf16[1,512,768]{2,1,0:T(8,128)(2,1)S(1)} %copy-done.3, f32[768]{0:T(1024)S(1)} %copy-done.21, f32[768]{0:T(1024)S(1)} %get-tuple-element.41, f32[512]{0:T(512)S(1)} %add_rsqrt_fusion, f32[512]{0:T(512)S(1)} %broadcast_multiply_fusion.4), kind=kOutput, calls=%fused_computation.27 | convolution fusion | flops 2420637696 | bytes 8660992 | tf_op jit(solution)/shard_map/td,tf->df/dot_general | solution.py:667
  328.6 4.6 %convolution_convert_fusion = bf16[3072,768]{1,0:T(8,128)(2,1)} fusion(bf16[512,3072]{1,0:T(8,128)(2,1)S(1)} %copy-done.23, bf16[1,512,768]{2,1,0:T(8,128)(2,1)S(1)} %copy-done.9), kind=kOutput, calls=%fused_computation.26 | convolution fusion | flops 2418278400 | bytes 8650752 | tf_op jit(solution)/shard_map/tf,td->fd/dot_general | solution.py:664
  333.2 60.6 %sum_grads.1 = (f32[24,3328]{1,0:T(8,128)}, f32[24,3072]{1,0:T(8,128)}, f32[96,768]{1,0:T(8,128)}) custom-call(bf16[32,24,3328]{2,1,0:T(8,128)(2,1)} %bitcast.171, bf16[32,24,3072]{2,1,0:T(8,128)(2,1)} %bitcast.175, bf16[32,96,768]{2,1,0:T(8,128)(2,1)} %bitcast.176), custom_call_target="tpu_custom_call" | custom-call | tf_op jit(solution)/shard_map/sum_grads/pallas_call | solution.py:389
  393.8 1.7 slice_reduce_fusion
  398.3 1.5 slice.194
  (132 shorter events, 24.2 us)
Async XLA Ops:
  0.6 20.5 %copy-start.19 = (bf16[24,768]{1,0:T(8,128)(2,1)S(1)}, bf16[24,768]{1,0:T(8,128)(2,1)}, u32[]{:S(2)}) copy-start(bf16[24,768]{1,0:T(8,128)(2,1)} %param.26) | copy-start | bytes 110596
  19.7 6.9 %copy-start.18 = (s32[1,2048]{1,0:T(1,128)}, s32[1,2048]{1,0:T(1,128)S(1)}, u32[]{:S(2)}) copy-start(s32[1,2048]{1,0:T(1,128)S(1)} %all-gather.doc_row) | copy-start | bytes 24580
  23.1 94.6 %copy-start.4 = (f32[512,192]{1,0:T(8,128)}, f32[512,192]{1,0:T(8,128)S(1)}, u32[]{:S(2)}) copy-start(f32[512,192]{1,0:T(8,128)S(1)} %copy.116) | copy-start | bytes 1179652
  25.6 59.1 %copy-start.8 = (bf16[1,512,768]{2,1,0:T(8,128)(2,1)S(1)}, bf16[1,512,768]{2,1,0:T(8,128)(2,1)}, u32[]{:S(2)}) copy-start(bf16[1,512,768]{2,1,0:T(8,128)(2,1)} %param.19) | copy-start | bytes 2359300
  83.7 183.7 %copy-start.20 = (f32[768]{0:T(1024)}, f32[768]{0:T(1024)S(1)}, u32[]{:S(2)}) copy-start(f32[768]{0:T(1024)S(1)} %get-tuple-element.40) | copy-start | bytes 9220
  84.6 5.5 %copy-start.2 = (bf16[1,512,768]{2,1,0:T(8,128)(2,1)S(1)}, bf16[1,512,768]{2,1,0:T(8,128)(2,1)}, u32[]{:S(2)}) copy-start(bf16[1,512,768]{2,1,0:T(8,128)(2,1)} %param.16) | copy-start | bytes 2359300
  113.8 2.4 copy-start
  117.8 3.6 copy-start.6
  117.8 3.6 copy-start.7
  240.7 5.7 %copy-start.1 = (bf16[4,512,768]{2,1,0:T(8,128)(2,1)S(1)}, bf16[4,512,768]{2,1,0:T(8,128)(2,1)}, u32[]{:S(2)}) copy-start(bf16[4,512,768]{2,1,0:T(8,128)(2,1)} %exchange.3) | copy-start | bytes 9437188
  249.8 1.8 copy-start.5
  249.8 1.8 copy-start.11
  257.6 3.7 copy-start.3
  261.3 25.7 %slice-start.4 = ((s8[4718592]{0:T(1024)(128)(4,1)}), s8[4194304]{0:T(1024)(128)(4,1)S(1)}, s32[]{:S(2)}) async-start(s8[4718592]{0:T(1024)(128)(4,1)} %bitcast.209), calls=%async_computation.4 | async-start | bytes 8388608
  261.3 37.2 %slice-start = ((s8[5111808]{0:T(1024)(128)(4,1)}), s8[4194304]{0:T(1024)(128)(4,1)S(1)}, s32[]{:S(2)}) async-start(s8[5111808]{0:T(1024)(128)(4,1)} %bitcast.195), calls=%async_computation | async-start | bytes 8388608
  261.3 39.1 %slice-start.2 = ((s8[4718592]{0:T(1024)(128)(4,1)}), s8[4194304]{0:T(1024)(128)(4,1)S(1)}, s32[]{:S(2)}) async-start(s8[4718592]{0:T(1024)(128)(4,1)} %bitcast.206), calls=%async_computation.2 | async-start | bytes 8388608
  267.4 19.6 %copy-start.9 = (bf16[1,512,768]{2,1,0:T(8,128)(2,1)S(1)}, bf16[1,512,768]{2,1,0:T(8,128)(2,1)}, u32[]{:S(2)}) copy-start(bf16[1,512,768]{2,1,0:T(8,128)(2,1)} %param.19) | copy-start | bytes 2359300
  267.4 19.6 %slice-start.5 = ((s8[4718592]{0:T(1024)(128)(4,1)}), s8[524288]{0:T(1024)(128)(4,1)S(1)}, s32[]{:S(2)}) async-start(s8[4718592]{0:T(1024)(128)(4,1)} %bitcast.209), calls=%async_computation.5 | async-start | bytes 1048576
  267.4 31.2 %slice-start.1 = ((s8[5111808]{0:T(1024)(128)(4,1)}), s8[917504]{0:T(1024)(128)(4,1)S(1)}, s32[]{:S(2)}) async-start(s8[5111808]{0:T(1024)(128)(4,1)} %bitcast.195), calls=%async_computation.1 | async-start | bytes 1835008
  267.4 33.0 %slice-start.3 = ((s8[4718592]{0:T(1024)(128)(4,1)}), s8[524288]{0:T(1024)(128)(4,1)S(1)}, s32[]{:S(2)}) async-start(s8[4718592]{0:T(1024)(128)(4,1)} %bitcast.206), calls=%async_computation.3 | async-start | bytes 1048576
  287.0 8.9 %copy-start.22 = (bf16[512,3072]{1,0:T(8,128)(2,1)}, bf16[512,3072]{1,0:T(8,128)(2,1)S(1)}, u32[]{:S(2)}) copy-start(bf16[512,3072]{1,0:T(8,128)(2,1)S(1)} %get-tuple-element.52) | copy-start | bytes 9437188
  295.9 4.5 %copy-start.24 = (bf16[512,3072]{1,0:T(8,128)(2,1)}, bf16[512,3072]{1,0:T(8,128)(2,1)S(1)}, u32[]{:S(2)}) copy-start(bf16[512,3072]{1,0:T(8,128)(2,1)S(1)} %get-tuple-element.84) | copy-start | bytes 9437188
  295.9 2.6 copy-start.14
  300.4 2.7 copy-start.10
  306.3 6.4 %copy-start.12 = (bf16[768,1]{1,0:T(8,128)(2,1)S(1)}, bf16[768,1]{1,0:T(8,128)(2,1)}, u32[]{:S(2)}) copy-start(bf16[768,1]{1,0:T(8,128)(2,1)} %reshape.252) | copy-start | bytes 4612
  306.3 6.4 %copy-start.13 = (bf16[768,768]{1,0:T(8,128)(2,1)S(1)}, bf16[768,768]{1,0:T(8,128)(2,1)}, u32[]{:S(2)}) copy-start(bf16[768,768]{1,0:T(8,128)(2,1)} %convolution_convert_fusion.3) | copy-start | bytes 3538948
  306.3 6.4 %copy-start.15 = (bf16[768,3]{1,0:T(8,128)(2,1)S(1)}, bf16[768,3]{1,0:T(8,128)(2,1)}, u32[]{:S(2)}) copy-start(bf16[768,3]{1,0:T(8,128)(2,1)} %reshape_reshape.8) | copy-start | bytes 13828
  312.7 9.2 %copy-start.21 = (f32[768]{0:T(1024)S(1)}, f32[768]{0:T(1024)}, u32[]{:S(2)}) copy-start(f32[768]{0:T(1024)} %copy-done.20) | copy-start | bytes 9220
  321.9 6.7 %copy-start.23 = (bf16[512,3072]{1,0:T(8,128)(2,1)S(1)}, bf16[512,3072]{1,0:T(8,128)(2,1)}, u32[]{:S(2)}) copy-start(bf16[512,3072]{1,0:T(8,128)(2,1)} %copy-done.22) | copy-start | bytes 9437188
  393.8 8.2 %copy-start.17 = (f32[24,3072]{1,0:T(8,128)S(1)}, f32[24,3072]{1,0:T(8,128)}, u32[]{:S(2)}) copy-start(f32[24,3072]{1,0:T(8,128)} %get-tuple-element.114) | copy-start | bytes 884740
  393.8 8.9 %copy-start.16 = (f32[96,768]{1,0:T(8,128)S(1)}, f32[96,768]{1,0:T(8,128)}, u32[]{:S(2)}) copy-start(f32[96,768]{1,0:T(8,128)} %get-tuple-element.116) | copy-start | bytes 884740
